TPU v7x, 32 devices: a whole 2x2x4 slice. The times are simulated.
32 devices in a mesh: ctx: 8 (over y, x, core), grp: 4 (over z).
Axes of the slice: x: 2, y: 2, z: 4, core: 2. Of those that a mesh axis runs over, the one named last changes fastest.
Arguments:
- queries: bfloat16 [8192, 128], P(('grp', 'ctx')), parts along dimension 0, may hold values from -6 to 6
- keys: bfloat16 [8192, 128], P(('grp', 'ctx')), parts along dimension 0, may hold values from -6 to 6
- values: bfloat16 [8192, 128], P(('grp', 'ctx')), parts along dimension 0, may hold values from -6 to 6
- grad_out: bfloat16 [8192, 128], P(('grp', 'ctx')), parts along dimension 0, may hold values from -6 to 6
Outputs:
- output: bfloat16 [8192, 128], P(('grp', 'ctx')), parts along dimension 0
- grad_query: bfloat16 [8192, 128], P(('grp', 'ctx')), parts along dimension 0
- grad_key: bfloat16 [8192, 128], P(('grp', 'ctx')), parts along dimension 0
- grad_value: bfloat16 [8192, 128], P(('grp', 'ctx')), parts along dimension 0
There are 4 independent parts, one for each index of `grp`. A program takes and returns all parts, laid end to end along the dimension named above; each array names one. Nothing has to cross between parts.
All inputs are finite; a program needn't handle non-finite values.
Results may differ from a plain program's by a relative error of at most 0.025.
Values may be sent and summed in bfloat16 or wider, within the bound.
A program may use at most 64 MiB of HBM per device.

v0:
```python
import math

import jax
import jax.numpy as jnp
from jax import lax
from jax.sharding import PartitionSpec as P


def block_rows():
    return 512


def forward_piece(state, queries, query_pos, range_low, range_high, keys, values, factor):
    count = keys.shape[0]
    size = block_rows()
    last_pos = query_pos[-1]

    def forward_one_block(carry, index):
        first = index * size
        needed = (first <= last_pos) & (first + size > range_low) & (first < range_high)

        def forward_compute(inner):
            peak, total, accum = inner
            key_block = lax.dynamic_slice_in_dim(keys, first, size, 0)
            value_block = lax.dynamic_slice_in_dim(values, first, size, 0)
            key_pos = first + jnp.arange(size, dtype=jnp.int32)
            scores = jnp.dot(queries, key_block.T, preferred_element_type=jnp.float32) * factor
            allowed = (
                (key_pos[None, :] <= query_pos[:, None])
                & (key_pos[None, :] >= range_low)
                & (key_pos[None, :] < range_high)
            )
            new_peak = jnp.maximum(peak, jnp.max(jnp.where(allowed, scores, -1e30), axis=1))
            shifted = jnp.where(
                allowed, jnp.exp(jnp.where(allowed, scores - new_peak[:, None], 0.0)), 0.0
            )
            decay = jnp.exp(peak - new_peak)
            total = total * decay + jnp.sum(shifted, axis=1)
            accum = accum * decay[:, None] + jnp.dot(
                shifted.astype(jnp.bfloat16), value_block, preferred_element_type=jnp.float32
            )
            return (new_peak, total, accum)

        def forward_keep(inner):
            return inner

        return (lax.cond(needed, forward_compute, forward_keep, carry), None)

    state, _ = lax.scan(forward_one_block, state, jnp.arange(count // size, dtype=jnp.int32))
    return state


def query_side(
    grad_query, queries, query_pos, grad_rows, log_total, row_delta, keys, values, factor
):
    count = keys.shape[0]
    size = block_rows()

    def query_one_block(carry, index):
        first = index * size
        needed = first <= query_pos[-1]

        def query_compute(inner):
            key_block = lax.dynamic_slice_in_dim(keys, first, size, 0)
            value_block = lax.dynamic_slice_in_dim(values, first, size, 0)
            key_pos = first + jnp.arange(size, dtype=jnp.int32)
            scores = jnp.dot(queries, key_block.T, preferred_element_type=jnp.float32) * factor
            allowed = key_pos[None, :] <= query_pos[:, None]
            probs = jnp.where(
                allowed, jnp.exp(jnp.where(allowed, scores - log_total[:, None], 0.0)), 0.0
            )
            grad_probs = jnp.dot(grad_rows, value_block.T, preferred_element_type=jnp.float32)
            grad_scores = (probs * (grad_probs - row_delta[:, None])).astype(jnp.bfloat16)
            return inner + jnp.dot(grad_scores, key_block, preferred_element_type=jnp.float32)

        def query_keep(inner):
            return inner

        return (lax.cond(needed, query_compute, query_keep, carry), None)

    grad_query, _ = lax.scan(
        query_one_block, grad_query, jnp.arange(count // size, dtype=jnp.int32)
    )
    return grad_query


def key_side(state, keys, values, key_pos, query_rows, grad_rows, all_totals, all_deltas, factor):
    count = query_rows.shape[0]
    size = block_rows()
    contract = (((0,), (0,)), ((), ()))

    def key_one_block(carry, index):
        first = index * size
        needed = first + size - 1 >= key_pos[0]

        def key_compute(inner):
            grad_keys, grad_values = inner
            query_block = lax.dynamic_slice_in_dim(query_rows, first, size, 0)
            grad_block = lax.dynamic_slice_in_dim(grad_rows, first, size, 0)
            query_pos = first + jnp.arange(size, dtype=jnp.int32)
            block_total = lax.dynamic_slice_in_dim(all_totals, first, size, 0)
            block_delta = lax.dynamic_slice_in_dim(all_deltas, first, size, 0)
            scores = jnp.dot(query_block, keys.T, preferred_element_type=jnp.float32) * factor
            allowed = key_pos[None, :] <= query_pos[:, None]
            probs = jnp.where(
                allowed, jnp.exp(jnp.where(allowed, scores - block_total[:, None], 0.0)), 0.0
            )
            grad_probs = jnp.dot(grad_block, values.T, preferred_element_type=jnp.float32)
            grad_scores = (probs * (grad_probs - block_delta[:, None])).astype(jnp.bfloat16)
            grad_values = grad_values + lax.dot_general(
                probs.astype(jnp.bfloat16), grad_block, contract, preferred_element_type=jnp.float32
            )
            grad_keys = grad_keys + lax.dot_general(
                grad_scores, query_block, contract, preferred_element_type=jnp.float32
            )
            return (grad_keys, grad_values)

        def key_keep(inner):
            return inner

        return (lax.cond(needed, key_compute, key_keep, carry), None)

    state, _ = lax.scan(key_one_block, state, jnp.arange(count // size, dtype=jnp.int32))
    return state


def shards(queries, keys, values, grad_out):
    rows = queries.shape[0]
    width = queries.shape[1]
    factor = 1.0 / math.sqrt(width)
    device_index = lax.axis_index("ctx")
    first_row = device_index * rows
    own_pos = first_row + jnp.arange(rows, dtype=jnp.int32)
    own_end = first_row + rows
    query_sets = ((queries, own_pos, jnp.int32(0), own_end),)
    initial = tuple(
        (
            (
                jnp.full((rows,), -1e30, jnp.float32),
                jnp.zeros((rows,), jnp.float32),
                jnp.zeros((rows, width), jnp.float32),
            )
            for member in query_sets
        )
    )
    piece = (
        lax.all_gather(keys, "ctx", axis=0, tiled=True),
        lax.all_gather(values, "ctx", axis=0, tiled=True),
    )
    key_rows = piece[0]
    value_rows = piece[1]
    states = tuple(
        (
            forward_piece(
                state, member[0], member[1], member[2], member[3], key_rows, value_rows, factor
            )
            for state, member in zip(initial, query_sets)
        )
    )
    peak, total, accum = states[0]
    log_total = peak + jnp.log(total)
    output = (accum / total[:, None]).astype(jnp.bfloat16)
    row_delta = jnp.sum(grad_out.astype(jnp.float32) * output.astype(jnp.float32), axis=1)
    all_totals, all_deltas = (
        lax.all_gather(log_total, "ctx", axis=0, tiled=True),
        lax.all_gather(row_delta, "ctx", axis=0, tiled=True),
    )
    zeros = jnp.zeros((rows, width), jnp.float32)
    piece = (
        lax.all_gather(keys, "ctx", axis=0, tiled=True),
        lax.all_gather(values, "ctx", axis=0, tiled=True),
    )
    grad_query = query_side(
        zeros, queries, own_pos, grad_out, log_total, row_delta, piece[0], piece[1], factor
    )
    piece = (
        lax.all_gather(queries, "ctx", axis=0, tiled=True),
        lax.all_gather(grad_out, "ctx", axis=0, tiled=True),
    )
    grad_keys, grad_values = key_side(
        (zeros, zeros), keys, values, own_pos, piece[0], piece[1], all_totals, all_deltas, factor
    )
    grad_query = (grad_query * factor).astype(jnp.bfloat16)
    grad_key = (grad_keys * factor).astype(jnp.bfloat16)
    grad_value = grad_values.astype(jnp.bfloat16)
    return (output, grad_query, grad_key, grad_value)


def solution(mesh):
    placed = (
        P(("grp", "ctx"), None),
        P(("grp", "ctx"), None),
        P(("grp", "ctx"), None),
        P(("grp", "ctx"), None),
    )
    return jax.shard_map(
        shards,
        mesh=mesh,
        in_specs=placed,
        out_specs=(
            P(("grp", "ctx"), None),
            P(("grp", "ctx"), None),
            P(("grp", "ctx"), None),
            P(("grp", "ctx"), None),
        ),
        check_vma=False,
    )
```

profile of v0, /device:TPU:0, one launch (start us, length us, event | category | flops | bytes accessed | tf_op | source)
XLA Modules:
  0.0 102.5 jit_solution(10976671070494809208)
XLA Ops:
  0.6 0.6 slice.15
  1.2 11.7 %all_gather.20 = bf16[2048,128]{1,0:T(8,128)(2,1)S(1)} all-gather(bf16[256,128]{1,0:T(8,128)(2,1)} %param.17), channel_id=1, replica_groups=mesh['ctx'=8,'grp'=4] {'ctx'}, dimensions={0}, use_global_device_ids=true | all-gather | bytes 589824 | tf_op jit(solution)/shard_map/all_gather | solution.py:147
  13.0 9.5 %all_gather.21 = bf16[2048,128]{1,0:T(8,128)(2,1)S(1)} all-gather(bf16[256,128]{1,0:T(8,128)(2,1)S(1)} %copy-done.1), channel_id=1, replica_groups=mesh['ctx'=8,'grp'=4] {'ctx'}, dimensions={0}, use_global_device_ids=true | all-gather | bytes 589824 | tf_op jit(solution)/shard_map/all_gather | solution.py:148
  22.5 0.8 copy-done.2
  23.3 8.8 %while.46 = (s32[]{:T(128)}, f32[256]{0:T(256)S(1)}, f32[256]{0:T(256)S(1)}, f32[256,128]{1,0:T(8,128)S(1)}, s32[4]{0:T(128)S(1)}, /*index=5*/s32[]{:T(128)}, s3...) while((s32[]{:T(128)}, f32[256]{0:T(256)S(1)}, ...), condition=%wide.region_5.6_spmd.clone, body=%wide.region_0.5_spmd.clone.sunk | while | flops 69798664 | bytes 2197913 | solution.py:49
  23.3 0.6 dynamic_slice.66
  25.2 1.3 %conditional.9 = ((f32[256]{0:T(256)S(1)}, f32[256]{0:T(256)S(1)}, f32[256,128]{1,0:T(8,128)S(1)})) conditional(s32[]{:T(128)} %convert_element_type.77, (f32[256]{0:T(256)S(1)}, f32[256]{0:T(256)S(1)}, f32[256,128]{1,0:T(8,128)S(1)}) %tuple.102, (s32[]{:T(128)}, s32[]{:T(128)}, s32[]{:T(128)}, bf16[2048,128]{1,0:T(8,128)(2,1)S(1)}, ...), branch_computations={%region_1.1_spmd, %region_2.4_spmd} | conditional | flops 69798656 | bytes 2196570 | solution.py:47
  25.2 0.3 select_reduce_fusion
  25.9 0.6 convolution_add_fusion
  26.5 0.6 dynamic_slice.66
  28.4 0.6 dynamic_slice.66
  30.2 0.6 dynamic_slice.66
  32.1 0.7 multiply_reduce_fusion
  32.9 10.9 %while.44 = (s32[]{:T(128)}, f32[256,128]{1,0:T(8,128)S(1)}, s32[4]{0:T(128)S(1)}, s32[256]{0:T(256)S(1)}, bf16[2048,128]{1,0:T(8,128)(2,1)S(1)}, /*index=5*/bf1...) while((s32[]{:T(128)}, f32[256,128]{1,0:T(8,128)S(1)}, ...), condition=%wide.region_10.11_spmd, body=%wide.region_7.10_spmd.sunk | while | flops 101745152 | bytes 1843485 | solution.py:81
  32.9 0.6 dynamic_slice.64
  34.1 0.6 slice.18
  35.4 0.7 conditional.7
  35.7 0.4 fusion.28
  36.2 0.6 dynamic_slice.64
  37.4 0.6 slice.18
  38.7 0.6 dynamic_slice.64
  40.0 0.6 slice.18
  41.3 0.6 dynamic_slice.64
  42.5 0.6 slice.18
  43.8 13.8 %all-gather.1 = f32[8,1,256]{2,1,0:T(1,128)S(1)} all-gather(f32[1,1,256]{2,1,0:T(1,128)S(1)} %bitcast.45), channel_id=1, replica_groups=mesh['ctx'=8,'grp'=4] {'ctx'}, dimensions={0}, use_global_device_ids=true | all-gather | bytes 9216 | tf_op jit(solution)/shard_map/all_gather | solution.py:166
  57.6 9.1 %all-gather = f32[8,1,256]{2,1,0:T(1,128)S(1)} all-gather(f32[1,1,256]{2,1,0:T(1,128)S(1)} %bitcast.48), channel_id=1, replica_groups=mesh['ctx'=8,'grp'=4] {'ctx'}, dimensions={0}, use_global_device_ids=true | all-gather | bytes 9216 | tf_op jit(solution)/shard_map/all_gather | solution.py:165
  66.6 8.7 %all_gather.22 = bf16[2048,128]{1,0:T(8,128)(2,1)S(1)} all-gather(bf16[256,128]{1,0:T(8,128)(2,1)S(1)} %get-tuple-element.906), channel_id=1, replica_groups=mesh['ctx'=8,'grp'=4] {'ctx'}, dimensions={0}, use_global_device_ids=true | all-gather | bytes 589824 | tf_op jit(solution)/shard_map/all_gather | solution.py:177
  75.3 10.0 %all_gather.24 = bf16[2048,128]{1,0:T(8,128)(2,1)S(1)} all-gather(bf16[256,128]{1,0:T(8,128)(2,1)S(1)} %get-tuple-element.900), channel_id=1, replica_groups=mesh['ctx'=8,'grp'=4] {'ctx'}, dimensions={0}, use_global_device_ids=true | all-gather | bytes 589824 | tf_op jit(solution)/shard_map/all_gather | solution.py:178
  85.4 0.8 copy-done.3
  86.2 14.9 %while.45 = (s32[]{:T(128)}, f32[256,128]{1,0:T(8,128)S(1)}, f32[256,128]{1,0:T(8,128)S(1)}, s32[4]{0:T(128)S(1)}, s32[256]{0:T(256)S(1)}, /*index=5*/bf16[2048,...) while((s32[]{:T(128)}, f32[256,128]{1,0:T(8,128)S(1)}, ...), condition=%wide.region_14.15_spmd, body=%wide.region_11.14_spmd.sunk | while | flops 135463424 | bytes 2771309 | solution.py:123
  86.2 0.6 dynamic_slice.65
  87.4 0.5 slice.19
  88.6 1.3 %conditional.8 = ((f32[256,128]{1,0:T(8,128)S(1)}, f32[256,128]{1,0:T(8,128)S(1)})) conditional(s32[]{:T(128)} %convert_element_type.76, (f32[256,128]{1,0:T(8,128)S(1)}, f32[256,128]{1,0:T(8,128)S(1)}) %tuple.99, (s32[256]{0:T(256)S(1)}, s32[]{:T(128)}, bf16[2048,128]{1,0:T(8,128)(2,1)S(1)}, bf16[256,128]{1,0:T(8,128)(2,1)S(1)}, ...), branch_computations={%region_12.12_spmd, %region_13.13_spmd} | conditional | flops 135463424 | bytes 2771022 | solution.py:121
  89.1 0.5 fusion.50
  89.9 0.6 dynamic_slice.65
  91.2 0.5 slice.19
  92.3 1.3 %conditional.8 = ((f32[256,128]{1,0:T(8,128)S(1)}, f32[256,128]{1,0:T(8,128)S(1)})) conditional(s32[]{:T(128)} %convert_element_type.76, (f32[256,128]{1,0:T(8,128)S(1)}, f32[256,128]{1,0:T(8,128)S(1)}) %tuple.99, (s32[256]{0:T(256)S(1)}, s32[]{:T(128)}, bf16[2048,128]{1,0:T(8,128)(2,1)S(1)}, bf16[256,128]{1,0:T(8,128)(2,1)S(1)}, ...), branch_computations={%region_12.12_spmd, %region_13.13_spmd} | conditional | flops 135463424 | bytes 2771022 | solution.py:121
  92.8 0.5 fusion.50
  93.7 0.6 dynamic_slice.65
  94.9 0.5 slice.19
  96.1 1.3 %conditional.8 = ((f32[256,128]{1,0:T(8,128)S(1)}, f32[256,128]{1,0:T(8,128)S(1)})) conditional(s32[]{:T(128)} %convert_element_type.76, (f32[256,128]{1,0:T(8,128)S(1)}, f32[256,128]{1,0:T(8,128)S(1)}) %tuple.99, (s32[256]{0:T(256)S(1)}, s32[]{:T(128)}, bf16[2048,128]{1,0:T(8,128)(2,1)S(1)}, bf16[256,128]{1,0:T(8,128)(2,1)S(1)}, ...), branch_computations={%region_12.12_spmd, %region_13.13_spmd} | conditional | flops 135463424 | bytes 2771022 | solution.py:121
  96.6 0.5 fusion.50
  97.4 0.6 dynamic_slice.65
  98.7 0.5 slice.19
  99.8 1.3 %conditional.8 = ((f32[256,128]{1,0:T(8,128)S(1)}, f32[256,128]{1,0:T(8,128)S(1)})) conditional(s32[]{:T(128)} %convert_element_type.76, (f32[256,128]{1,0:T(8,128)S(1)}, f32[256,128]{1,0:T(8,128)S(1)}) %tuple.99, (s32[256]{0:T(256)S(1)}, s32[]{:T(128)}, bf16[2048,128]{1,0:T(8,128)(2,1)S(1)}, bf16[256,128]{1,0:T(8,128)(2,1)S(1)}, ...), branch_computations={%region_12.12_spmd, %region_13.13_spmd} | conditional | flops 135463424 | bytes 2771022 | solution.py:121
  100.3 0.5 fusion.50
  101.2 0.7 multiply_convert_fusion
  101.8 0.6 convert_element_type.50
  (56 shorter events, 3.7 us)
Async XLA Ops:
  1.2 11.7 %copy-start.1 = (bf16[256,128]{1,0:T(8,128)(2,1)S(1)}, bf16[256,128]{1,0:T(8,128)(2,1)}, u32[]{:S(2)}) copy-start(bf16[256,128]{1,0:T(8,128)(2,1)} %param.18) | copy-start | bytes 196612
  22.5 0.8 copy-start.2
  23.3 8.8 %copy-start = (bf16[256,128]{1,0:T(8,128)(2,1)S(1)}, bf16[256,128]{1,0:T(8,128)(2,1)}, u32[]{:S(2)}) copy-start(bf16[256,128]{1,0:T(8,128)(2,1)} %param.19) | copy-start | bytes 196612
  85.4 0.8 copy-start.3
where the time goes:
time: 103 us; the launch traced here: 102 us
  blocking collectives  62.8 us (61%)
  loops' own time  15.9 us (15%)
  local copies, waits for them, and re-layouts  14.6 us (14%)
  matrix products  6.02 us (6%)
  other arithmetic  2.42 us (2%)
    all_gather x1, blocking collectives, shards(): lax.all_gather(row_delta, 'ctx', axis=0, tiled=True)  13.8 us
    all_gather x1, blocking collectives, shards(): lax.all_gather(keys, 'ctx', axis=0, tiled=True)  11.7 us
    all_gather x1, blocking collectives, shards(): lax.all_gather(grad_out, 'ctx', axis=0, tiled=True)  10 us
    all_gather x1, blocking collectives, shards(): lax.all_gather(values, 'ctx', axis=0, tiled=True)  9.53 us
    all_gather x1, blocking collectives, shards(): lax.all_gather(log_total, 'ctx', axis=0, tiled=True)  9.06 us
    all_gather x1, blocking collectives, shards(): lax.all_gather(queries, 'ctx', axis=0, tiled=True)  8.66 us
    dynamic_slice x12, local copies, waits for them, and re-layouts, forward_piece(): lax.scan(forward_one_block, state, jnp.arange(count // size, dtype=jnp.in...  7.04 us
    another operation x1, loops' own time, key_side(): lax.scan(key_one_block, state, jnp.arange(count // size, dtype=jnp.int32))  5.31 us

commit v1 on v0

v1 whole, which is shorter than its diff:
```python
import functools
import math

import jax
import jax.numpy as jnp
from jax import lax
from jax.experimental import pallas as pl
from jax.experimental.pallas import tpu as pltpu
from jax.sharding import PartitionSpec as P

MESH = pl.DeviceIdType.MESH
LOWEST = -1e30
NT = (((1,), (1,)), ((), ()))


def flip(index, by, count):
    result = 0
    bit = 1
    while bit < count:
        both = (index // bit) % 2 + (by // bit) % 2
        result = result + (both % 2) * bit
        bit *= 2
    return result


def kernel(
    n, q_hbm, k_hbm, v_hbm, g_hbm, o_hbm, dq_hbm, dk_hbm, dv_hbm,
    own, slots, raw, graw, stats, peak, total, accum, dq, dk, dv, outs,
    load_sem, send_sem, recv_sem, relay_sem, stat_send, stat_recv, store_sem,
):
    rows, width = q_hbm.shape
    factor = 1.0 / math.sqrt(width)
    scale = factor * math.log2(math.e)
    me = lax.axis_index("ctx")
    chips = n // 2
    chip, core = me // 2, me % 2
    sibling = chip * 2 + 1 - core
    Q, K, V, G = 0, 1, 2, 3

    loads = [
        pltpu.make_async_copy(src, own.at[i], load_sem.at[i])
        for i, src in enumerate((q_hbm, k_hbm, v_hbm, g_hbm))
    ]
    for load in loads:
        load.start()
    barrier = pltpu.get_barrier_semaphore()

    def greet(step, carry):
        other = (me + step) % n
        pl.semaphore_signal(barrier, inc=1, device_id={"ctx": other}, device_id_type=MESH)
        return carry

    lax.fori_loop(1, n, greet, 0)
    for load in loads:
        load.wait()
    pl.semaphore_wait(barrier, n - 1)

    def send_copy(part, other):
        above = (other > me).astype(jnp.int32)
        first = above * (K if part == 0 else V) + (1 - above) * (Q if part == 0 else G)
        return pltpu.make_async_remote_copy(
            src_ref=own.at[first],
            dst_ref=slots.at[me, part],
            send_sem=send_sem.at[other, part],
            recv_sem=recv_sem.at[me, part],
            device_id={"ctx": other},
            device_id_type=MESH,
        )

    def arrival(source, part):
        return pltpu.make_async_remote_copy(
            src_ref=slots.at[source, part],
            dst_ref=slots.at[source, part],
            send_sem=relay_sem.at[source, part],
            recv_sem=recv_sem.at[source, part],
            device_id={"ctx": sibling},
            device_id_type=MESH,
        )

    def send_all(step, carry):
        other = flip(chip, step, chips) * 2 + core
        send_copy(0, other).start()
        send_copy(1, other).start()
        return carry

    lax.fori_loop(1, chips, send_all, 0)
    send_copy(0, sibling).start()
    send_copy(1, sibling).start()

    def dot(a, b):
        return jnp.dot(a, b, preferred_element_type=jnp.float32)

    def dot_nt(a, b):
        return lax.dot_general(a, b, NT, preferred_element_type=jnp.float32)

    row = lax.broadcasted_iota(jnp.int32, (rows, rows), 0)
    col = lax.broadcasted_iota(jnp.int32, (rows, rows), 1)
    scores = jnp.where(col <= row, dot_nt(own[Q], own[K]) * scale, LOWEST)
    raw[me] = scores
    graw[me] = dot_nt(own[G], own[V])
    top = jnp.max(scores, axis=1, keepdims=True)
    probs = jnp.exp2(scores - top)
    peak[...] = jnp.broadcast_to(top, peak.shape)
    total[...] = jnp.broadcast_to(jnp.sum(probs, axis=1, keepdims=True), total.shape)
    accum[...] = dot(probs.astype(jnp.bfloat16), own[V])
    raw[n] = jnp.where(row <= col, dot_nt(own[K], own[Q]) * scale, LOWEST)
    graw[n] = dot_nt(own[V], own[G])

    def take(source):
        above = (source > me).astype(jnp.int32)
        left = own[above * K + (1 - above) * Q]
        right = own[above * V + (1 - above) * G]
        scores = dot_nt(left, slots[source, 0]) * scale
        raw[source] = scores
        graw[source] = dot_nt(right, slots[source, 1])

        @pl.when(source < me)
        def _():
            before = peak[...]
            s = raw[source]
            top = jnp.maximum(before, jnp.max(s, axis=1, keepdims=True))
            decay = jnp.exp2(before - top)
            probs = jnp.exp2(s - top[:, :1])
            peak[...] = top
            total[...] = total[...] * decay + jnp.sum(probs, axis=1, keepdims=True)
            accum[...] = accum[...] * decay[:, :1] + dot(
                probs.astype(jnp.bfloat16), slots[source, 1]
            )

    for part in range(2):
        arrival(sibling, part).wait_recv()
    take(sibling)

    def receive(step, carry):
        far = flip(chip, step, chips) * 2
        for part in range(2):
            arrival(far + core, part).wait_recv()
            arrival(far + core, part).start()
        take(far + core)
        for part in range(2):
            arrival(far + 1 - core, part).wait_recv()
        take(far + 1 - core)
        return carry

    lax.fori_loop(1, chips, receive, 0)

    log_total = peak[:, :1] + jnp.log2(total[:, :1])
    out = (accum[...] / total[:, :1]).astype(jnp.bfloat16)
    outs[0] = out
    delta = jnp.sum(own[G].astype(jnp.float32) * out.astype(jnp.float32), axis=1, keepdims=True)
    lane = lax.broadcasted_iota(jnp.int32, (rows, 128), 1)
    both = jnp.where(lane < 8, log_total, delta)
    stats[me] = jnp.transpose(both)[:16, :]
    store_out = pltpu.make_async_copy(outs.at[0], o_hbm, store_sem.at[0])
    store_out.start()

    def stat_copy(source, other):
        return pltpu.make_async_remote_copy(
            src_ref=stats.at[source],
            dst_ref=stats.at[source],
            send_sem=stat_send.at[other],
            recv_sem=stat_recv.at[source],
            device_id={"ctx": other},
            device_id_type=MESH,
        )

    def send_stats(other, carry):
        stat_copy(me, other).start()
        return carry

    lax.fori_loop(0, me, send_stats, 0)

    peak[...] = jnp.broadcast_to(log_total, peak.shape)
    total[...] = jnp.broadcast_to(delta, total.shape)

    def query_block(source, keys):
        probs = jnp.exp2(raw[source] - peak[:, :1])
        return dot((probs * (graw[source] - total[:, :1])).astype(jnp.bfloat16), keys)

    dq[...] = query_block(me, own[K])

    def query_step(source, carry):
        dq[...] += query_block(source, slots[source, 0])
        return carry

    lax.fori_loop(0, me, query_step, 0)
    outs[1] = (dq[...] * factor).astype(jnp.bfloat16)
    store_dq = pltpu.make_async_copy(outs.at[1], dq_hbm, store_sem.at[1])
    store_dq.start()

    def key_block(place, source, queries, grads):
        probs = jnp.exp2(raw[place] - stats[source, 0:1, :])
        gvalue = dot(probs.astype(jnp.bfloat16), grads)
        ds = (probs * (graw[place] - stats[source, 8:9, :])).astype(jnp.bfloat16)
        return dot(ds, queries), gvalue

    gk, gv = key_block(n, me, own[Q], own[G])
    dk[...] = gk
    dv[...] = gv

    def key_step(source, carry):
        stat_copy(source, sibling).wait_recv()
        gk, gv = key_block(source, source, slots[source, 0], slots[source, 1])
        dk[...] += gk
        dv[...] += gv
        return carry

    lax.fori_loop(me + 1, n, key_step, 0)
    outs[2] = (dk[...] * factor).astype(jnp.bfloat16)
    outs[3] = dv[...].astype(jnp.bfloat16)
    store_dk = pltpu.make_async_copy(outs.at[2], dk_hbm, store_sem.at[2])
    store_dv = pltpu.make_async_copy(outs.at[3], dv_hbm, store_sem.at[3])
    store_dk.start()
    store_dv.start()

    def drain(step, carry):
        far = flip(chip, step, chips) * 2 + core
        for part in range(2):
            send_copy(part, far).wait_send()
            arrival(far, part).wait_send()
        return carry

    lax.fori_loop(1, chips, drain, 0)
    for part in range(2):
        send_copy(part, sibling).wait_send()

    def drain_stats(other, carry):
        stat_copy(me, other).wait_send()
        return carry

    lax.fori_loop(0, me, drain_stats, 0)
    store_out.wait()
    store_dq.wait()
    store_dk.wait()
    store_dv.wait()


def shards(n, queries, keys, values, grad_out):
    rows, width = queries.shape
    shape = jax.ShapeDtypeStruct((rows, width), jnp.bfloat16)
    f32 = jnp.float32
    return pl.pallas_call(
        functools.partial(kernel, n),
        out_shape=(shape,) * 4,
        in_specs=[pl.BlockSpec(memory_space=pltpu.HBM)] * 4,
        out_specs=(pl.BlockSpec(memory_space=pltpu.HBM),) * 4,
        scratch_shapes=[
            pltpu.VMEM((4, rows, width), jnp.bfloat16),
            pltpu.VMEM((n, 2, rows, width), jnp.bfloat16),
            pltpu.VMEM((n + 1, rows, rows), f32),
            pltpu.VMEM((n + 1, rows, rows), f32),
            pltpu.VMEM((n, 16, rows), f32),
            pltpu.VMEM((rows, 128), f32),
            pltpu.VMEM((rows, 128), f32),
            pltpu.VMEM((rows, width), f32),
            pltpu.VMEM((rows, width), f32),
            pltpu.VMEM((rows, width), f32),
            pltpu.VMEM((rows, width), f32),
            pltpu.VMEM((4, rows, width), jnp.bfloat16),
            pltpu.SemaphoreType.DMA((4,)),
            pltpu.SemaphoreType.DMA((n, 2)),
            pltpu.SemaphoreType.DMA((n, 2)),
            pltpu.SemaphoreType.DMA((n, 2)),
            pltpu.SemaphoreType.DMA((n,)),
            pltpu.SemaphoreType.DMA((n,)),
            pltpu.SemaphoreType.DMA((4,)),
        ],
        compiler_params=pltpu.CompilerParams(
            collective_id=0,
            has_side_effects=True,
            vmem_limit_bytes=60 * 1024 * 1024,
        ),
    )(queries, keys, values, grad_out)


def solution(mesh):
    placed = P(("grp", "ctx"), None)
    return jax.shard_map(
        functools.partial(shards, mesh.shape["ctx"]),
        mesh=mesh,
        in_specs=(placed,) * 4,
        out_specs=(placed,) * 4,
        check_vma=False,
    )
```

time: 103 us -> 23.8 us (0.23)
  blocking collectives: 62.8 us -> 0 us
  Pallas kernels: 0 us -> 18.9 us
  loops' own time: 15.9 us -> 0 us
  local copies, waits for them, and re-layouts: 14.6 us -> 3.86 us
  matrix products: 6.02 us -> 0 us
  other arithmetic: 2.42 us -> 0 us
    all_gather x6 -> x0, blocking collectives: 62.8 us -> none  [the longest x1 13.8 us: shards(): lax.all_gather(row_delta, 'ctx', axis=0, tiled=True)]
    pallas_call x0 -> x1, Pallas kernels: none -> 18.9 us  [shards(): pl.pallas_call(functools.partial(kernel, n), out_shape=(shape,) * 4, in_s...]
    another operation x15 -> x0, loops' own time: 15.9 us -> none  [the longest x1 5.31 us: key_side(): lax.scan(key_one_block, state, jnp.arange(count // size, dtype=jnp.int32))]
    dynamic_slice x20 -> x0, local copies, waits for them, and re-layouts: 7.68 us -> none  [the longest x12 7.04 us: forward_piece(): lax.scan(forward_one_block, state, jnp.arange(count // size, dtype=jnp.in...]
    dot_general x16 -> x0, matrix products: 6.02 us -> none  [the longest x4 2.09 us: key_compute(): lax.dot_general(grad_scores, query_block, contract, preferred_element_typ...]
    slice x9 -> x0, local copies, waits for them, and re-layouts: 5.22 us -> none  [the longest x4 2.58 us: query_one_block(): needed = first <= query_pos[-1]]
    unnamed x8 -> x10, local copies, waits for them, and re-layouts: 1.63 us -> 3.86 us
    convert_element_type x2 -> x0, other arithmetic: 1.32 us -> none  [the longest x1 0.68 us: shards(): grad_key = (grad_keys * factor).astype(jnp.bfloat16)]
where the time goes in v1:
time: 23.8 us; the launch traced here: 23.4 us
  Pallas kernels  18.9 us (79%)
  local copies, waits for them, and re-layouts  3.86 us (16%)
  between operations  0.65 us (3%)
    pallas_call x1, Pallas kernels, shards(): pl.pallas_call(functools.partial(kernel, n), out_shape=(shape,) * 4, in_s...  18.9 us
    unnamed x10, local copies, waits for them, and re-layouts  3.86 us

profile of v1, /device:TPU:0, one launch (start us, length us, event | category | flops | bytes accessed | tf_op | source)
XLA Modules:
  0.0 23.4 jit_solution(10412713972750114644)
XLA Ops:
  0.6 18.9 %shard_map.75 = (bf16[256,128]{1,0:T(8,128)(2,1)}, bf16[256,128]{1,0:T(8,128)(2,1)}, bf16[256,128]{1,0:T(8,128)(2,1)}, bf16[256,128]{1,0:T(8,128)(2,1)}) custom-call(bf16[256,128]{1,0:T(8,128)(2,1)} %q_hbm.1, bf16[256,128]{1,0:T(8,128)(2,1)} %k_hbm.1, bf16[256,128]{1,0:T(8,128)(2,1)} %v_hbm.1, bf16[256,128]{1,0:T(8,128)(2,1)} %g_hbm.1), custom_call_target="tpu_custom_call" | custom-call | tf_op jit(solution)/shard_map/pallas_call | solution.py:242
  19.6 0.0 copy-start.2
  19.6 1.5 %copy.12 = bf16[256,128]{1,0:T(8,128)(2,1)} copy(bf16[256,128]{1,0:T(8,128)(2,1)} %get-tuple-element.8) | data formatting | bytes 131072
  21.1 0.0 copy-done.2
  21.1 0.0 copy-start.1
  21.1 0.6 %copy.13 = bf16[256,128]{1,0:T(8,128)(2,1)} copy(bf16[256,128]{1,0:T(8,128)(2,1)S(1)} %copy-done.2) | data formatting | bytes 131072
  21.7 0.2 copy-done.1
  21.9 0.0 copy-start
  21.9 0.6 %copy.14 = bf16[256,128]{1,0:T(8,128)(2,1)} copy(bf16[256,128]{1,0:T(8,128)(2,1)S(1)} %copy-done.1) | data formatting | bytes 131072
  22.6 0.2 copy-done
  22.8 0.6 %copy.15 = bf16[256,128]{1,0:T(8,128)(2,1)} copy(bf16[256,128]{1,0:T(8,128)(2,1)S(1)} %copy-done) | data formatting | bytes 131072
Async XLA Ops:
  19.6 1.5 %copy-start.2 = (bf16[256,128]{1,0:T(8,128)(2,1)S(1)}, bf16[256,128]{1,0:T(8,128)(2,1)}, u32[]{:S(2)}) copy-start(bf16[256,128]{1,0:T(8,128)(2,1)} %get-tuple-element.9) | copy-start | bytes 196612
  21.1 0.9 %copy-start.1 = (bf16[256,128]{1,0:T(8,128)(2,1)S(1)}, bf16[256,128]{1,0:T(8,128)(2,1)}, u32[]{:S(2)}) copy-start(bf16[256,128]{1,0:T(8,128)(2,1)} %get-tuple-element.10) | copy-start | bytes 196612
  21.9 0.9 %copy-start = (bf16[256,128]{1,0:T(8,128)(2,1)S(1)}, bf16[256,128]{1,0:T(8,128)(2,1)}, u32[]{:S(2)}) copy-start(bf16[256,128]{1,0:T(8,128)(2,1)} %get-tuple-element.11) | copy-start | bytes 196612

commit v2 on v1

--- a/solution.py
+++ b/solution.py
@@ -24,9 +24,9 @@
 
 
 def kernel(
-    n, q_hbm, k_hbm, v_hbm, g_hbm, o_hbm, dq_hbm, dk_hbm, dv_hbm,
-    own, slots, raw, graw, stats, peak, total, accum, dq, dk, dv, outs,
-    load_sem, send_sem, recv_sem, relay_sem, stat_send, stat_recv, store_sem,
+    n, q_hbm, k_hbm, v_hbm, g_hbm, o_ref, dq_ref, dk_ref, dv_ref,
+    own, slots, raw, graw, stats, peak, total, accum, dq, dk, dv,
+    load_sem, send_sem, recv_sem, relay_sem, stat_send, stat_recv,
 ):
     rows, width = q_hbm.shape
     factor = 1.0 / math.sqrt(width)
@@ -93,6 +93,9 @@
     def dot_nt(a, b):
         return lax.dot_general(a, b, NT, preferred_element_type=jnp.float32)
 
+    def fold(a):
+        return sum(a[:, i : i + 128] for i in range(0, rows, 128))
+
     row = lax.broadcasted_iota(jnp.int32, (rows, rows), 0)
     col = lax.broadcasted_iota(jnp.int32, (rows, rows), 1)
     scores = jnp.where(col <= row, dot_nt(own[Q], own[K]) * scale, LOWEST)
@@ -101,7 +104,7 @@
     top = jnp.max(scores, axis=1, keepdims=True)
     probs = jnp.exp2(scores - top)
     peak[...] = jnp.broadcast_to(top, peak.shape)
-    total[...] = jnp.broadcast_to(jnp.sum(probs, axis=1, keepdims=True), total.shape)
+    total[...] = fold(probs)
     accum[...] = dot(probs.astype(jnp.bfloat16), own[V])
     raw[n] = jnp.where(row <= col, dot_nt(own[K], own[Q]) * scale, LOWEST)
     graw[n] = dot_nt(own[V], own[G])
@@ -122,37 +125,10 @@
             decay = jnp.exp2(before - top)
             probs = jnp.exp2(s - top[:, :1])
             peak[...] = top
-            total[...] = total[...] * decay + jnp.sum(probs, axis=1, keepdims=True)
+            total[...] = total[...] * decay + fold(probs)
             accum[...] = accum[...] * decay[:, :1] + dot(
                 probs.astype(jnp.bfloat16), slots[source, 1]
             )
-
-    for part in range(2):
-        arrival(sibling, part).wait_recv()
-    take(sibling)
-
-    def receive(step, carry):
-        far = flip(chip, step, chips) * 2
-        for part in range(2):
-            arrival(far + core, part).wait_recv()
-            arrival(far + core, part).start()
-        take(far + core)
-        for part in range(2):
-            arrival(far + 1 - core, part).wait_recv()
-        take(far + 1 - core)
-        return carry
-
-    lax.fori_loop(1, chips, receive, 0)
-
-    log_total = peak[:, :1] + jnp.log2(total[:, :1])
-    out = (accum[...] / total[:, :1]).astype(jnp.bfloat16)
-    outs[0] = out
-    delta = jnp.sum(own[G].astype(jnp.float32) * out.astype(jnp.float32), axis=1, keepdims=True)
-    lane = lax.broadcasted_iota(jnp.int32, (rows, 128), 1)
-    both = jnp.where(lane < 8, log_total, delta)
-    stats[me] = jnp.transpose(both)[:16, :]
-    store_out = pltpu.make_async_copy(outs.at[0], o_hbm, store_sem.at[0])
-    store_out.start()
 
     def stat_copy(source, other):
         return pltpu.make_async_remote_copy(
@@ -168,10 +144,47 @@
         stat_copy(me, other).start()
         return carry
 
-    lax.fori_loop(0, me, send_stats, 0)
-
-    peak[...] = jnp.broadcast_to(log_total, peak.shape)
-    total[...] = jnp.broadcast_to(delta, total.shape)
+    def finish_rows():
+        ahead = jnp.sum(total[...], axis=1, keepdims=True)
+        log_total = peak[:, :1] + jnp.log2(ahead)
+        out = (accum[...] / ahead).astype(jnp.bfloat16)
+        o_ref[...] = out
+        product = own[G].astype(jnp.float32) * out.astype(jnp.float32)
+        delta = jnp.sum(product, axis=1, keepdims=True)
+        lane = lax.broadcasted_iota(jnp.int32, (rows, 128), 1)
+        both = jnp.where(lane < 4, log_total, delta)
+        stats[me] = jnp.transpose(both)[:8, :]
+        lax.fori_loop(0, me, send_stats, 0)
+        peak[...] = jnp.broadcast_to(log_total, peak.shape)
+        total[...] = jnp.broadcast_to(delta, total.shape)
+
+    last = 0
+    bit = 1
+    while bit < chips:
+        last = last + bit * (chip >= bit).astype(jnp.int32)
+        bit *= 2
+
+    def receive(step, carry):
+        far = flip(chip, step, chips) * 2
+
+        @pl.when(step > 0)
+        def _():
+            for part in range(2):
+                arrival(far + core, part).wait_recv()
+                arrival(far + core, part).start()
+            take(far + core)
+
+        for part in range(2):
+            arrival(far + 1 - core, part).wait_recv()
+        take(far + 1 - core)
+
+        @pl.when(step == last)
+        def _():
+            finish_rows()
+
+        return carry
+
+    lax.fori_loop(0, chips, receive, 0)
 
     def query_block(source, keys):
         probs = jnp.exp2(raw[source] - peak[:, :1])
@@ -184,14 +197,12 @@
         return carry
 
     lax.fori_loop(0, me, query_step, 0)
-    outs[1] = (dq[...] * factor).astype(jnp.bfloat16)
-    store_dq = pltpu.make_async_copy(outs.at[1], dq_hbm, store_sem.at[1])
-    store_dq.start()
+    dq_ref[...] = (dq[...] * factor).astype(jnp.bfloat16)
 
     def key_block(place, source, queries, grads):
         probs = jnp.exp2(raw[place] - stats[source, 0:1, :])
         gvalue = dot(probs.astype(jnp.bfloat16), grads)
-        ds = (probs * (graw[place] - stats[source, 8:9, :])).astype(jnp.bfloat16)
+        ds = (probs * (graw[place] - stats[source, 4:5, :])).astype(jnp.bfloat16)
         return dot(ds, queries), gvalue
 
     gk, gv = key_block(n, me, own[Q], own[G])
@@ -206,12 +217,8 @@
         return carry
 
     lax.fori_loop(me + 1, n, key_step, 0)
-    outs[2] = (dk[...] * factor).astype(jnp.bfloat16)
-    outs[3] = dv[...].astype(jnp.bfloat16)
-    store_dk = pltpu.make_async_copy(outs.at[2], dk_hbm, store_sem.at[2])
-    store_dv = pltpu.make_async_copy(outs.at[3], dv_hbm, store_sem.at[3])
-    store_dk.start()
-    store_dv.start()
+    dk_ref[...] = (dk[...] * factor).astype(jnp.bfloat16)
+    dv_ref[...] = dv[...].astype(jnp.bfloat16)
 
     def drain(step, carry):
         far = flip(chip, step, chips) * 2 + core
@@ -229,41 +236,47 @@
         return carry
 
     lax.fori_loop(0, me, drain_stats, 0)
-    store_out.wait()
-    store_dq.wait()
-    store_dk.wait()
-    store_dv.wait()
+
+
+def deliver(*refs):
+    sources, targets, sem = refs[:4], refs[4:8], refs[8]
+    copies = [
+        pltpu.make_async_copy(source, target, sem.at[i])
+        for i, (source, target) in enumerate(zip(sources, targets))
+    ]
+    for copy in copies:
+        copy.start()
+    for copy in copies:
+        copy.wait()
 
 
 def shards(n, queries, keys, values, grad_out):
     rows, width = queries.shape
     shape = jax.ShapeDtypeStruct((rows, width), jnp.bfloat16)
     f32 = jnp.float32
-    return pl.pallas_call(
+    results = pl.pallas_call(
         functools.partial(kernel, n),
-        out_shape=(shape,) * 4,
+        out_shape=(pltpu.VMEM((rows, width), jnp.bfloat16),) * 4,
         in_specs=[pl.BlockSpec(memory_space=pltpu.HBM)] * 4,
-        out_specs=(pl.BlockSpec(memory_space=pltpu.HBM),) * 4,
+        out_specs=(pl.BlockSpec(memory_space=pltpu.VMEM),) * 4,
         scratch_shapes=[
             pltpu.VMEM((4, rows, width), jnp.bfloat16),
             pltpu.VMEM((n, 2, rows, width), jnp.bfloat16),
             pltpu.VMEM((n + 1, rows, rows), f32),
             pltpu.VMEM((n + 1, rows, rows), f32),
-            pltpu.VMEM((n, 16, rows), f32),
+            pltpu.VMEM((n, 8, rows), f32),
             pltpu.VMEM((rows, 128), f32),
             pltpu.VMEM((rows, 128), f32),
             pltpu.VMEM((rows, width), f32),
             pltpu.VMEM((rows, width), f32),
             pltpu.VMEM((rows, width), f32),
             pltpu.VMEM((rows, width), f32),
-            pltpu.VMEM((4, rows, width), jnp.bfloat16),
             pltpu.SemaphoreType.DMA((4,)),
             pltpu.SemaphoreType.DMA((n, 2)),
             pltpu.SemaphoreType.DMA((n, 2)),
             pltpu.SemaphoreType.DMA((n, 2)),
             pltpu.SemaphoreType.DMA((n,)),
             pltpu.SemaphoreType.DMA((n,)),
-            pltpu.SemaphoreType.DMA((4,)),
         ],
         compiler_params=pltpu.CompilerParams(
             collective_id=0,
@@ -271,6 +284,13 @@
             vmem_limit_bytes=60 * 1024 * 1024,
         ),
     )(queries, keys, values, grad_out)
+    return pl.pallas_call(
+        deliver,
+        out_shape=(shape,) * 4,
+        in_specs=[pl.BlockSpec(memory_space=pltpu.VMEM)] * 4,
+        out_specs=(pl.BlockSpec(memory_space=pltpu.HBM),) * 4,
+        scratch_shapes=[pltpu.SemaphoreType.DMA((4,))],
+    )(*results)
 
 
 def solution(mesh):

time: 23.8 us -> 23 us (0.966)
  local copies, waits for them, and re-layouts: 3.86 us -> 2.49 us
  Pallas kernels: 18.9 us -> 19.7 us
    unnamed x10 -> x8, local copies, waits for them, and re-layouts: 3.86 us -> 2.49 us
    pallas_call x1 -> x2, Pallas kernels: 18.9 us -> 19.7 us  [the longest x1 18 us: shards(): pl.pallas_call(functools.partial(kernel, n), out_shape=(pltpu.VMEM((rows,...]
where the time goes in v2:
time: 23 us; the launch traced here: 22.8 us
  Pallas kernels  19.7 us (86%)
  local copies, waits for them, and re-layouts  2.49 us (11%)
  between operations  0.65 us (3%)
    pallas_call x1, Pallas kernels, shards(): pl.pallas_call(functools.partial(kernel, n), out_shape=(pltpu.VMEM((rows,...  18 us
    unnamed x8, local copies, waits for them, and re-layouts  2.49 us
    pallas_call x1, Pallas kernels, shards(): pl.pallas_call(deliver, out_shape=(shape,) * 4, in_specs=[pl.BlockSpec(me...  1.66 us

profile of v2, /device:TPU:0, one launch (start us, length us, event | category | flops | bytes accessed | tf_op | source)
XLA Modules:
  0.0 22.8 jit_solution(7570538385543859808)
XLA Ops:
  0.6 18.0 %shard_map.75 = (bf16[256,128]{1,0:T(8,128)(2,1)S(1)}, bf16[256,128]{1,0:T(8,128)(2,1)S(1)}, bf16[256,128]{1,0:T(8,128)(2,1)S(1)}, bf16[256,128]{1,0:T(8,128)(2,1)S(1)}) custom-call(bf16[256,128]{1,0:T(8,128)(2,1)} %q_hbm.1, bf16[256,128]{1,0:T(8,128)(2,1)} %k_hbm.1, bf16[256,128]{1,0:T(8,128)(2,1)} %v_hbm.1, bf16[256,128]{1,0:T(8,128)(2,1)} %g_hbm.1), custom_call_target="tpu_custom_call" | custom-call | tf_op jit(solution)/shard_map/pallas_call | solution.py:257
  18.6 0.0 copy-start
  18.6 0.6 %copy-done = bf16[256,128]{1,0:T(8,128)(2,1)} copy-done((bf16[256,128]{1,0:T(8,128)(2,1)}, bf16[256,128]{1,0:T(8,128)(2,1)S(1)}, u32[]{:S(2)}) %copy-start) | copy-done | bytes 65560
  19.3 0.0 copy-start.1
  19.3 0.6 %copy-done.1 = bf16[256,128]{1,0:T(8,128)(2,1)} copy-done((bf16[256,128]{1,0:T(8,128)(2,1)}, bf16[256,128]{1,0:T(8,128)(2,1)S(1)}, u32[]{:S(2)}) %copy-start.1) | copy-done | bytes 65560
  19.9 0.0 copy-start.2
  19.9 0.6 %copy-done.2 = bf16[256,128]{1,0:T(8,128)(2,1)} copy-done((bf16[256,128]{1,0:T(8,128)(2,1)}, bf16[256,128]{1,0:T(8,128)(2,1)S(1)}, u32[]{:S(2)}) %copy-start.2) | copy-done | bytes 65560
  20.5 0.0 copy-start.3
  20.5 0.6 %copy-done.3 = bf16[256,128]{1,0:T(8,128)(2,1)} copy-done((bf16[256,128]{1,0:T(8,128)(2,1)}, bf16[256,128]{1,0:T(8,128)(2,1)S(1)}, u32[]{:S(2)}) %copy-start.3) | copy-done | bytes 65560
  21.1 1.7 %shard_map.76 = (bf16[256,128]{1,0:T(8,128)(2,1)}, bf16[256,128]{1,0:T(8,128)(2,1)}, bf16[256,128]{1,0:T(8,128)(2,1)}, bf16[256,128]{1,0:T(8,128)(2,1)}) custom-call(bf16[256,128]{1,0:T(8,128)(2,1)} %copy-done, bf16[256,128]{1,0:T(8,128)(2,1)} %copy-done.1, bf16[256,128]{1,0:T(8,128)(2,1)} %copy-done.2, bf16[256,128]{1,0:T(8,128)(2,1)} %copy-done.3), custom_call_target="tpu_custom_call" | custom-call | tf_op jit(solution)/shard_map/pallas_call | solution.py:287
Async XLA Ops:
  18.6 0.6 %copy-start = (bf16[256,128]{1,0:T(8,128)(2,1)}, bf16[256,128]{1,0:T(8,128)(2,1)S(1)}, u32[]{:S(2)}) copy-start(bf16[256,128]{1,0:T(8,128)(2,1)S(1)} %get-tuple-element.8.refs_0_) | copy-start | bytes 196612
  19.3 0.6 %copy-start.1 = (bf16[256,128]{1,0:T(8,128)(2,1)}, bf16[256,128]{1,0:T(8,128)(2,1)S(1)}, u32[]{:S(2)}) copy-start(bf16[256,128]{1,0:T(8,128)(2,1)S(1)} %get-tuple-element.9.refs_1_) | copy-start | bytes 196612
  19.9 0.6 %copy-start.2 = (bf16[256,128]{1,0:T(8,128)(2,1)}, bf16[256,128]{1,0:T(8,128)(2,1)S(1)}, u32[]{:S(2)}) copy-start(bf16[256,128]{1,0:T(8,128)(2,1)S(1)} %get-tuple-element.10.refs_2_) | copy-start | bytes 196612
  20.5 0.6 %copy-start.3 = (bf16[256,128]{1,0:T(8,128)(2,1)}, bf16[256,128]{1,0:T(8,128)(2,1)S(1)}, u32[]{:S(2)}) copy-start(bf16[256,128]{1,0:T(8,128)(2,1)S(1)} %get-tuple-element.11.refs_3_) | copy-start | bytes 196612

commit v3 on v2

--- a/solution.py
+++ b/solution.py
@@ -96,6 +96,9 @@
     def fold(a):
         return sum(a[:, i : i + 128] for i in range(0, rows, 128))
 
+    def wide(a):
+        return jnp.concatenate([a] * (rows // 128), axis=1)
+
     row = lax.broadcasted_iota(jnp.int32, (rows, rows), 0)
     col = lax.broadcasted_iota(jnp.int32, (rows, rows), 1)
     scores = jnp.where(col <= row, dot_nt(own[Q], own[K]) * scale, LOWEST)
@@ -123,10 +126,10 @@
             s = raw[source]
             top = jnp.maximum(before, jnp.max(s, axis=1, keepdims=True))
             decay = jnp.exp2(before - top)
-            probs = jnp.exp2(s - top[:, :1])
+            probs = jnp.exp2(s - wide(top))
             peak[...] = top
             total[...] = total[...] * decay + fold(probs)
-            accum[...] = accum[...] * decay[:, :1] + dot(
+            accum[...] = accum[...] * decay + dot(
                 probs.astype(jnp.bfloat16), slots[source, 1]
             )
 
@@ -187,8 +190,8 @@
     lax.fori_loop(0, chips, receive, 0)
 
     def query_block(source, keys):
-        probs = jnp.exp2(raw[source] - peak[:, :1])
-        return dot((probs * (graw[source] - total[:, :1])).astype(jnp.bfloat16), keys)
+        probs = jnp.exp2(raw[source] - wide(peak[...]))
+        return dot((probs * (graw[source] - wide(total[...]))).astype(jnp.bfloat16), keys)
 
     dq[...] = query_block(me, own[K])
 
@@ -290,6 +293,7 @@
         in_specs=[pl.BlockSpec(memory_space=pltpu.VMEM)] * 4,
         out_specs=(pl.BlockSpec(memory_space=pltpu.HBM),) * 4,
         scratch_shapes=[pltpu.SemaphoreType.DMA((4,))],
+        compiler_params=pltpu.CompilerParams(vmem_limit_bytes=2 * 1024 * 1024),
     )(*results)
 
 

time: 23 us -> 19.1 us (0.83)
  local copies, waits for them, and re-layouts: 2.49 us -> 0 us
  Pallas kernels: 19.7 us -> 18.3 us
    unnamed x8 -> x0, local copies, waits for them, and re-layouts: 2.49 us -> none
    pallas_call x1, Pallas kernels: 1.66 us -> 0.73 us  [shards(): pl.pallas_call(deliver, out_shape=(shape,) * 4, in_specs=[pl.BlockSpec(me...]
    pallas_call x1, Pallas kernels: 18 us -> 17.6 us  [shards(): pl.pallas_call(functools.partial(kernel, n), out_shape=(pltpu.VMEM((rows,...]
where the time goes in v3:
time: 19.1 us; the launch traced here: 19 us
  Pallas kernels  18.3 us (96%)
  between operations  0.64 us (3%)
    pallas_call x1, Pallas kernels, shards(): pl.pallas_call(functools.partial(kernel, n), out_shape=(pltpu.VMEM((rows,...  17.6 us
    pallas_call x1, Pallas kernels, shards(): pl.pallas_call(deliver, out_shape=(shape,) * 4, in_specs=[pl.BlockSpec(me...  0.73 us

profile of v3, /device:TPU:0, one launch (start us, length us, event | category | flops | bytes accessed | tf_op | source)
XLA Modules:
  0.0 19.0 jit_solution(1289146409510875197)
XLA Ops:
  0.6 17.6 %shard_map.75 = (bf16[256,128]{1,0:T(8,128)(2,1)S(1)}, bf16[256,128]{1,0:T(8,128)(2,1)S(1)}, bf16[256,128]{1,0:T(8,128)(2,1)S(1)}, bf16[256,128]{1,0:T(8,128)(2,1)S(1)}) custom-call(bf16[256,128]{1,0:T(8,128)(2,1)} %q_hbm.1, bf16[256,128]{1,0:T(8,128)(2,1)} %k_hbm.1, bf16[256,128]{1,0:T(8,128)(2,1)} %v_hbm.1, bf16[256,128]{1,0:T(8,128)(2,1)} %g_hbm.1), custom_call_target="tpu_custom_call" | custom-call | tf_op jit(solution)/shard_map/pallas_call | solution.py:260
  18.2 0.7 %shard_map.76 = (bf16[256,128]{1,0:T(8,128)(2,1)}, bf16[256,128]{1,0:T(8,128)(2,1)}, bf16[256,128]{1,0:T(8,128)(2,1)}, bf16[256,128]{1,0:T(8,128)(2,1)}) custom-call(bf16[256,128]{1,0:T(8,128)(2,1)S(1)} %get-tuple-element.8.refs_0_, bf16[256,128]{1,0:T(8,128)(2,1)S(1)} %get-tuple-element.9.refs_1_, bf16[256,128]{1,0:T(8,128)(2,1)S(1)} %get-tuple-element.10.refs_2_, ...), custom_call_target="tpu_custom_call" | custom-call | tf_op jit(solution)/shard_map/pallas_call | solution.py:290

commit v4 on v3

--- a/solution.py
+++ b/solution.py
@@ -26,7 +26,7 @@
 def kernel(
     n, q_hbm, k_hbm, v_hbm, g_hbm, o_ref, dq_ref, dk_ref, dv_ref,
     own, slots, raw, graw, stats, peak, total, accum, dq, dk, dv,
-    load_sem, send_sem, recv_sem, relay_sem, stat_send, stat_recv,
+    load_sem, send_sem, recv_sem, relay_sem, onward_sem, forward_sem, stat_send, stat_recv,
 ):
     rows, width = q_hbm.shape
     factor = 1.0 / math.sqrt(width)
@@ -50,10 +50,29 @@
         pl.semaphore_signal(barrier, inc=1, device_id={"ctx": other}, device_id_type=MESH)
         return carry
 
-    lax.fori_loop(1, n, greet, 0)
-    for load in loads:
-        load.wait()
-    pl.semaphore_wait(barrier, n - 1)
+    square = chips == 4
+    if square:
+        across = flip(chip, 3, chips) * 2 + core
+        for other in (sibling, flip(chip, 1, 4) * 2 + core, flip(chip, 2, 4) * 2 + core):
+            pl.semaphore_signal(barrier, inc=1, device_id={"ctx": other}, device_id_type=MESH)
+
+        @pl.when(chip != 3)
+        def _():
+            pl.semaphore_signal(barrier, inc=1, device_id={"ctx": across}, device_id_type=MESH)
+
+        for load in loads:
+            load.wait()
+        pl.semaphore_wait(barrier, 3 + (chip != 0).astype(jnp.int32))
+
+        @pl.when(chip == 1)
+        def _():
+            pl.semaphore_signal(onward_sem, inc=1, device_id={"ctx": core}, device_id_type=MESH)
+
+    else:
+        lax.fori_loop(1, n, greet, 0)
+        for load in loads:
+            load.wait()
+        pl.semaphore_wait(barrier, n - 1)
 
     def send_copy(part, other):
         above = (other > me).astype(jnp.int32)
@@ -83,9 +102,49 @@
         send_copy(1, other).start()
         return carry
 
-    lax.fori_loop(1, chips, send_all, 0)
-    send_copy(0, sibling).start()
-    send_copy(1, sibling).start()
+    def forward():
+        return pltpu.make_async_remote_copy(
+            src_ref=slots.at[core, 1],
+            dst_ref=slots.at[core, 1],
+            send_sem=forward_sem,
+            recv_sem=recv_sem.at[core, 1],
+            device_id={"ctx": 6 + core},
+            device_id_type=MESH,
+        )
+
+    def send_to(*copies):
+        for part, other in copies:
+            send_copy(part, other * 2 + core).start()
+
+    def send_sibling():
+        send_copy(0, sibling).start()
+        send_copy(1, sibling).start()
+
+    if square:
+
+        @pl.when(chip == 0)
+        def _():
+            send_to((0, 1), (1, 1), (0, 2), (1, 2))
+            send_sibling()
+
+        @pl.when(chip == 1)
+        def _():
+            send_to((0, 0), (1, 0), (0, 3), (1, 3), (0, 2), (1, 2))
+            send_sibling()
+
+        @pl.when(chip == 2)
+        def _():
+            send_to((0, 3), (1, 3), (0, 0), (1, 0))
+            send_sibling()
+
+        @pl.when(chip == 3)
+        def _():
+            send_to((0, 2), (1, 2), (0, 1), (1, 1), (0, 0), (1, 0))
+            send_sibling()
+
+    else:
+        lax.fori_loop(1, chips, send_all, 0)
+        send_sibling()
 
     def dot(a, b):
         return jnp.dot(a, b, preferred_element_type=jnp.float32)
@@ -111,6 +170,20 @@
     accum[...] = dot(probs.astype(jnp.bfloat16), own[V])
     raw[n] = jnp.where(row <= col, dot_nt(own[K], own[Q]) * scale, LOWEST)
     graw[n] = dot_nt(own[V], own[G])
+    if square:
+
+        @pl.when(chip == 0)
+        def _():
+            pl.semaphore_wait(onward_sem, 1)
+            send_to((0, 3))
+
+        @pl.when(chip == 2)
+        def _():
+            arrival(core, 1).wait_recv()
+            forward().start()
+            arrival(core, 1).start()
+            send_to((0, 1), (1, 1))
+
 
     def take(source):
         above = (source > me).astype(jnp.int32)
@@ -167,21 +240,32 @@
         last = last + bit * (chip >= bit).astype(jnp.int32)
         bit *= 2
 
-    def receive(step, carry):
+    def receive(event, carry):
+        step = event
+        if square:
+            step = event + ((event == 1).astype(jnp.int32) - (event == 2).astype(jnp.int32)) * (
+                1 - chip % 2
+            )
         far = flip(chip, step, chips) * 2
 
         @pl.when(step > 0)
         def _():
-            for part in range(2):
-                arrival(far + core, part).wait_recv()
-                arrival(far + core, part).start()
+            arrival(far + core, 0).wait_recv()
+            arrival(far + core, 0).start()
+            handled = square & (chip == 2) & (step == 2)
+
+            @pl.when(jnp.logical_not(handled))
+            def _():
+                arrival(far + core, 1).wait_recv()
+                arrival(far + core, 1).start()
+
             take(far + core)
 
         for part in range(2):
             arrival(far + 1 - core, part).wait_recv()
         take(far + 1 - core)
 
-        @pl.when(step == last)
+        @pl.when(event == last)
         def _():
             finish_rows()
 
@@ -226,11 +310,22 @@
     def drain(step, carry):
         far = flip(chip, step, chips) * 2 + core
         for part in range(2):
-            send_copy(part, far).wait_send()
             arrival(far, part).wait_send()
+        send_copy(0, far).wait_send()
+
+        @pl.when(jnp.logical_not(square & (chip == 0) & (step == 3)))
+        def _():
+            send_copy(1, far).wait_send()
+
         return carry
 
     lax.fori_loop(1, chips, drain, 0)
+    if square:
+
+        @pl.when(chip == 2)
+        def _():
+            forward().wait_send()
+
     for part in range(2):
         send_copy(part, sibling).wait_send()
 
@@ -278,6 +373,8 @@
             pltpu.SemaphoreType.DMA((n, 2)),
             pltpu.SemaphoreType.DMA((n, 2)),
             pltpu.SemaphoreType.DMA((n, 2)),
+            pltpu.SemaphoreType.REGULAR,
+            pltpu.SemaphoreType.DMA,
             pltpu.SemaphoreType.DMA((n,)),
             pltpu.SemaphoreType.DMA((n,)),
         ],

time: 19.1 us -> 18.1 us (0.948)
  Pallas kernels: 18.3 us -> 17.3 us
    pallas_call x1, Pallas kernels: 17.6 us -> 16.6 us  [shards(): pl.pallas_call(functools.partial(kernel, n), out_shape=(pltpu.VMEM((rows,...]
where the time goes in v4:
time: 18.1 us; the launch traced here: 17.9 us
  Pallas kernels  17.3 us (96%)
  between operations  0.64 us (4%)
    pallas_call x1, Pallas kernels, shards(): pl.pallas_call(functools.partial(kernel, n), out_shape=(pltpu.VMEM((rows,...  16.6 us
    pallas_call x1, Pallas kernels, shards(): pl.pallas_call(deliver, out_shape=(shape,) * 4, in_specs=[pl.BlockSpec(me...  0.73 us

profile of v4, /device:TPU:0, one launch (start us, length us, event | category | flops | bytes accessed | tf_op | source)
XLA Modules:
  0.0 17.9 jit_solution(3332983966234849957)
XLA Ops:
  0.6 16.6 %shard_map.75 = (bf16[256,128]{1,0:T(8,128)(2,1)S(1)}, bf16[256,128]{1,0:T(8,128)(2,1)S(1)}, bf16[256,128]{1,0:T(8,128)(2,1)S(1)}, bf16[256,128]{1,0:T(8,128)(2,1)S(1)}) custom-call(bf16[256,128]{1,0:T(8,128)(2,1)} %q_hbm.1, bf16[256,128]{1,0:T(8,128)(2,1)} %k_hbm.1, bf16[256,128]{1,0:T(8,128)(2,1)} %v_hbm.1, bf16[256,128]{1,0:T(8,128)(2,1)} %g_hbm.1), custom_call_target="tpu_custom_call" | custom-call | tf_op jit(solution)/shard_map/pallas_call | solution.py:355
  17.2 0.7 %shard_map.76 = (bf16[256,128]{1,0:T(8,128)(2,1)}, bf16[256,128]{1,0:T(8,128)(2,1)}, bf16[256,128]{1,0:T(8,128)(2,1)}, bf16[256,128]{1,0:T(8,128)(2,1)}) custom-call(bf16[256,128]{1,0:T(8,128)(2,1)S(1)} %get-tuple-element.8.refs_0_, bf16[256,128]{1,0:T(8,128)(2,1)S(1)} %get-tuple-element.9.refs_1_, bf16[256,128]{1,0:T(8,128)(2,1)S(1)} %get-tuple-element.10.refs_2_, ...), custom_call_target="tpu_custom_call" | custom-call | tf_op jit(solution)/shard_map/pallas_call | solution.py:387

commit v5 on v4

--- a/solution.py
+++ b/solution.py
@@ -124,7 +124,7 @@
 
         @pl.when(chip == 0)
         def _():
-            send_to((0, 1), (1, 1), (0, 2), (1, 2))
+            send_to((0, 2), (1, 2), (0, 1), (1, 1))
             send_sibling()
 
         @pl.when(chip == 1)

time: 18.1 us -> 18.1 us (level)
  no operation moved by 1% of the time
where the time goes in v5:
time: 18.1 us; the launch traced here: 17.9 us
  Pallas kernels  17.3 us (96%)
  between operations  0.64 us (4%)
    pallas_call x1, Pallas kernels, shards(): pl.pallas_call(functools.partial(kernel, n), out_shape=(pltpu.VMEM((rows,...  16.6 us
    pallas_call x1, Pallas kernels, shards(): pl.pallas_call(deliver, out_shape=(shape,) * 4, in_specs=[pl.BlockSpec(me...  0.73 us

profile of v5, /device:TPU:0, one launch (start us, length us, event | category | flops | bytes accessed | tf_op | source)
XLA Modules:
  0.0 17.9 jit_solution(12797852397481761036)
XLA Ops:
  0.6 16.6 %shard_map.75 = (bf16[256,128]{1,0:T(8,128)(2,1)S(1)}, bf16[256,128]{1,0:T(8,128)(2,1)S(1)}, bf16[256,128]{1,0:T(8,128)(2,1)S(1)}, bf16[256,128]{1,0:T(8,128)(2,1)S(1)}) custom-call(bf16[256,128]{1,0:T(8,128)(2,1)} %q_hbm.1, bf16[256,128]{1,0:T(8,128)(2,1)} %k_hbm.1, bf16[256,128]{1,0:T(8,128)(2,1)} %v_hbm.1, bf16[256,128]{1,0:T(8,128)(2,1)} %g_hbm.1), custom_call_target="tpu_custom_call" | custom-call | tf_op jit(solution)/shard_map/pallas_call | solution.py:355
  17.2 0.7 %shard_map.76 = (bf16[256,128]{1,0:T(8,128)(2,1)}, bf16[256,128]{1,0:T(8,128)(2,1)}, bf16[256,128]{1,0:T(8,128)(2,1)}, bf16[256,128]{1,0:T(8,128)(2,1)}) custom-call(bf16[256,128]{1,0:T(8,128)(2,1)S(1)} %get-tuple-element.8.refs_0_, bf16[256,128]{1,0:T(8,128)(2,1)S(1)} %get-tuple-element.9.refs_1_, bf16[256,128]{1,0:T(8,128)(2,1)S(1)} %get-tuple-element.10.refs_2_, ...), custom_call_target="tpu_custom_call" | custom-call | tf_op jit(solution)/shard_map/pallas_call | solution.py:387
